TPU v7x, 32 devices: a whole 2x2x4 slice. The times are simulated.
32 devices in a mesh: dp: 2 (over y), expert: 16 (over z, x, core).
Axes of the slice: x: 2, y: 2, z: 4, core: 2. Of those that a mesh axis runs over, the one named last changes fastest.
Arguments:
- latent: bfloat16 [4096, 4096], P(('dp', 'expert')), may hold values from -6 to 6
- dout: bfloat16 [4096, 4096], P(('dp', 'expert')), may hold values from -6 to 6
- routes: int32 [4096, 2], P(('dp', 'expert')), may hold values from 0 to 63, as said below
- gate_w: float32 [4096, 2], P(('dp', 'expert')), may hold values from 0.1 to 1
- norm_gain: float32 [4096], replicated, may hold values from 0.1 to 1.9
- w_gate_up: bfloat16 [16, 4096, 256], P('expert', 'dp'), may hold values from -0.09375 to 0.09375
- w_down: bfloat16 [16, 128, 4096], P('expert', None, 'dp'), may hold values from -0.1875 to 0.1875
Outputs:
- d_latent: bfloat16 [4096, 4096], P(('dp', 'expert'))
- grad_gate_up: bfloat16 [16, 4096, 256], P('expert', 'dp')
- grad_down: bfloat16 [16, 128, 4096], P('expert', None, 'dp')
Inputs may be any that keep to these rules, and one draw needn't show every extreme that they name: `routes`: each patch names two different experts, at most one of them below 2. The patches of one device name no expert below 2 more than 4 times, and in every draw some expert below 2 is named exactly 4 times by the patches of every device of one index of dp.
All inputs are finite; a program needn't handle non-finite values.
Results may differ from a plain program's by a relative error of at most 0.013.
Values may be sent and summed in bfloat16 or wider, within the bound.
A program may use at most 64 MiB of HBM per device.

v0:
```python
import jax
import jax.numpy as jnp
from jax import lax
from jax.sharding import PartitionSpec as P

SLICES = 8
CAP = 4


EPS = 1e-06


def expert_pass(rows_in, rows_dy, wgu, wd):
    hid = wd.shape[0]
    pre = jnp.dot(rows_in, wgu, preferred_element_type=jnp.float32)
    gate = pre[:, :hid]
    up = pre[:, hid:]
    sig = jax.nn.sigmoid(gate)
    act = gate * sig
    hidden = (act * up).astype(jnp.bfloat16)
    dh = lax.dot_general(rows_dy, wd, (((1,), (1,)), ((), ())), preferred_element_type=jnp.float32)
    d_up = dh * act
    d_gate = dh * up * sig * (1.0 + gate * (1.0 - sig))
    d_pre = jnp.concatenate([d_gate, d_up], axis=1).astype(jnp.bfloat16)
    return (hidden, d_pre)


def body(latent, dout, routes, gate_w, norm_gain, w_gate_up, w_down):
    width = latent.shape[1]
    members = lax.axis_size("expert")
    groups = members // SLICES
    values = latent.astype(jnp.float32)
    inverse = lax.rsqrt(jnp.mean(values * values, axis=1, keepdims=True) + EPS)
    scaled = values * inverse
    expert_in = (scaled * norm_gain[None, :]).astype(jnp.bfloat16)
    inside = routes < groups
    chosen = jnp.sum(jnp.where(inside, routes, 0), axis=1)
    present = jnp.any(inside, axis=1)
    weight = jnp.sum(jnp.where(inside, gate_w, jnp.float32(0.0)), axis=1)
    grad_scale = (weight[:, None] * dout.astype(jnp.float32)).astype(jnp.bfloat16)
    onehot = (
        (chosen[:, None] == jnp.arange(groups, dtype=jnp.int32)[None, :]) & present[:, None]
    ).astype(jnp.int32)
    slot = jnp.sum((jnp.cumsum(onehot, axis=0) - 1) * onehot, axis=1)
    target = chosen * CAP + slot
    select = (
        (target[None, :] == jnp.arange(groups * CAP, dtype=jnp.int32)[:, None]) & present[None, :]
    ).astype(jnp.bfloat16)
    send_in = (
        jnp.dot(select, expert_in, preferred_element_type=jnp.float32)
        .astype(jnp.bfloat16)
        .reshape(groups, CAP, width)
    )
    send_dy = (
        jnp.dot(select, grad_scale, preferred_element_type=jnp.float32)
        .astype(jnp.bfloat16)
        .reshape(groups, CAP, width)
    )
    full_gu, full_down = (
        lax.all_gather(w_gate_up, "dp", axis=1, tiled=True),
        lax.all_gather(w_down, "dp", axis=2, tiled=True),
    )
    wgu = full_gu[0]
    wd = full_down[0]
    wide_in = jnp.repeat(send_in, SLICES, axis=0)
    wide_dy = jnp.repeat(send_dy, SLICES, axis=0)
    got_in, got_dy = (
        lax.all_to_all(wide_in, "expert", split_axis=0, concat_axis=0, tiled=True),
        lax.all_to_all(wide_dy, "expert", split_axis=0, concat_axis=0, tiled=True),
    )
    rows_in = got_in.reshape(-1, width)
    rows_dy = got_dy.reshape(-1, width)
    hidden, d_pre = expert_pass(rows_in, rows_dy, wgu, wd)
    part_gu = lax.dot_general(
        rows_in, d_pre, (((0,), (0,)), ((), ())), preferred_element_type=jnp.float32
    )
    part_d = lax.dot_general(
        hidden, rows_dy, (((0,), (0,)), ((), ())), preferred_element_type=jnp.float32
    )
    back = lax.dot_general(
        d_pre, wgu, (((1,), (1,)), ((), ())), preferred_element_type=jnp.float32
    ).astype(jnp.bfloat16)
    grad_gu, grad_d = (
        lax.psum_scatter(
            part_gu[None].astype(jnp.bfloat16), "dp", scatter_dimension=1, tiled=True
        ).astype(jnp.float32),
        lax.psum_scatter(
            part_d[None].astype(jnp.bfloat16), "dp", scatter_dimension=2, tiled=True
        ).astype(jnp.float32),
    )
    home = lax.all_to_all(
        back.reshape(members, CAP, width), "expert", split_axis=0, concat_axis=0, tiled=True
    )
    summed = jnp.sum(home.reshape(groups, SLICES, CAP, width).astype(jnp.float32), axis=1).astype(
        jnp.bfloat16
    )
    d_in = lax.dot_general(
        select,
        summed.reshape(groups * CAP, width),
        (((0,), (0,)), ((), ())),
        preferred_element_type=jnp.float32,
    )
    grad_in = d_in * norm_gain[None, :]
    d_latent = inverse * (grad_in - scaled * jnp.mean(grad_in * scaled, axis=1, keepdims=True))
    return (
        d_latent.astype(jnp.bfloat16),
        grad_gu.astype(jnp.bfloat16),
        grad_d.astype(jnp.bfloat16),
    )


def solution(mesh):
    placed = (
        P(("dp", "expert"), None),
        P(("dp", "expert"), None),
        P(("dp", "expert"), None),
        P(("dp", "expert"), None),
        P(),
        P("expert", "dp", None),
        P("expert", None, "dp"),
    )
    return jax.shard_map(
        body,
        mesh=mesh,
        in_specs=placed,
        out_specs=(P(("dp", "expert"), None), P("expert", "dp", None), P("expert", None, "dp")),
        check_vma=False,
    )
```

profile of v0, /device:TPU:0, one launch (start us, length us, event | category | flops | bytes accessed | tf_op | source)
XLA Modules:
  0.0 132.6 jit_solution(8362228009213369047)
XLA Ops:
  7.2 0.0 all-gather.5.cloned.1.call-start
  7.2 0.0 copy-start
  7.2 0.7 all-gather.5.cloned.1.call-update
  7.9 0.8 copy.10
  8.7 0.1 fusion.37
  8.8 0.1 select_reduce_fusion.2
  8.9 0.1 fusion.21
  9.0 0.8 copy.12
  9.8 0.2 reduce_window_sum.11
  10.0 0.0 copy-start.3
  10.0 0.2 select_reduce_fusion.1
  10.2 0.1 select_reduce_fusion
  10.3 1.6 %convolution_convert_fusion.4 = bf16[8,4096]{1,0:T(8,128)(2,1)S(1)} fusion(bf16[128,4096]{1,0:T(8,128)(2,1)} %param.8, f32[128]{0:T(128)S(1)} %select_reduce_fusion, s32[128]{0:T(128)S(1)} %multiply_add_fusion, pred[128]{0:T(512)(128)(4,1)S(1)} %fusion.37), kind=kOutput, calls=%fused_computation.7 | convolution fusion | flops 9996288 | bytes 1115264 | tf_op jit(solution)/shard_map/dot_general | solution.py:55
  11.9 1.0 broadcast_in_dim.14
  12.9 7.4 %all-to-all-start = ((bf16[16,4,4096]{2,1,0:T(4,128)(2,1)}), bf16[16,4,4096]{2,1,0:T(4,128)(2,1)S(1)}, u32[]{:S(2)}, u32[]{:S(2)}) async-start(bf16[16,4,4096]{2,1,0:T(4,128)(2,1)} %bitcast), calls=%async_computation | async-start | bytes 1048576 | tf_op jit(solution)/shard_map/all_to_all | solution.py:69
  20.3 0.0 copy-done
  20.3 0.3 fusion.10
  20.6 0.0 copy-done.3
  20.6 0.4 convolution_convert_fusion.3
  21.1 13.7 %all-to-all-done = bf16[16,4,4096]{2,1,0:T(4,128)(2,1)S(1)} async-done(((bf16[16,4,4096]{2,1,0:T(4,128)(2,1)}), bf16[16,4,4096]{2,1,0:T(4,128)(2,1)S(1)}, u32[]{:S(2)}, u32[]{:S(2)}) %all-to-all-start) | async-done | bytes 524320 | tf_op jit(solution)/shard_map/all_to_all | solution.py:69
  34.8 1.0 broadcast_in_dim.15
  35.8 4.1 %all-to-all-start.1 = ((bf16[16,4,4096]{2,1,0:T(4,128)(2,1)}), bf16[16,4,4096]{2,1,0:T(4,128)(2,1)S(1)}, u32[]{:S(2)}, u32[]{:S(2)}) async-start(bf16[16,4,4096]{2,1,0:T(4,128)(2,1)} %bitcast.2), calls=%async_computation.1 | async-start | bytes 1048576 | tf_op jit(solution)/shard_map/all_to_all | solution.py:68
  39.9 0.0 all-gather.3.cloned.1.call-start
  39.9 0.7 all-gather.3.cloned.1.call-update
  40.6 0.0 reduce-scatter.5.cloned.1.call-start
  40.7 0.1 reshape.60
  40.8 13.5 %all-to-all-done.1 = bf16[16,4,4096]{2,1,0:T(4,128)(2,1)S(1)} async-done(((bf16[16,4,4096]{2,1,0:T(4,128)(2,1)}), bf16[16,4,4096]{2,1,0:T(4,128)(2,1)S(1)}, u32[]{:S(2)}, u32[]{:S(2)}) %all-to-all-start.1) | async-done | bytes 524320 | tf_op jit(solution)/shard_map/all_to_all | solution.py:68
  54.3 0.1 reshape.63
  54.4 0.0 copy-start.2
  54.5 0.0 all-gather.5.cloned.1.call-done
  54.5 2.3 %fusion.12 = f32[64,256]{1,0:T(8,128)S(1)} fusion(bf16[64,4096]{1,0:T(8,128)(2,1)S(1)} %reshape.63, bf16[1,4096,256]{2,1,0:T(8,128)(2,1)} %all-gather.5.cloned.1.call-done), kind=kOutput, calls=%fused_computation.20 | convolution fusion | flops 134217728 | bytes 2686976 | tf_op jit(solution)/shard_map/dot_general | solution.py:15
  56.8 1.5 %fusion.1 = bf16[1,128,4096]{2,1,0:T(8,128)(2,1)} fusion(bf16[64,4096]{1,0:T(8,128)(2,1)S(1)} %reshape.60, f32[64,256]{1,0:T(8,128)S(1)} %fusion.12), kind=kOutput, calls=%fused_computation.4 | convolution fusion | flops 67682304 | bytes 1638400 | tf_op jit(solution)/shard_map/dot_general | solution.py:77
  58.2 0.0 copy-done.2
  58.2 0.0 reduce-scatter.5.cloned.1.call-update
  58.3 0.0 reduce-scatter.3.cloned.1.call-start
  58.3 10.0 %all-gather.3.cloned.1.call-done = bf16[1,128,4096]{2,1,0:T(8,128)(2,1)} async-done(((bf16[1,128,2048]{2,1,0:T(8,128)(2,1)}), bf16[1,128,4096]{2,1,0:T(8,128)(2,1)}) %all-gather.3.cloned.1.call-update) | async-done | bytes 1048592 | tf_op jit(solution)/shard_map/all_gather | solution.py:61
  68.3 1.7 %multiply_convert_fusion.4 = (bf16[64,128]{1,0:T(8,128)(2,1)S(1)}, bf16[64,128]{1,0:T(8,128)(2,1)S(1)}) fusion(f32[64,256]{1,0:T(8,128)S(1)} %fusion.12, bf16[64,4096]{1,0:T(8,128)(2,1)S(1)} %reshape.60, bf16[1,128,4096]{2,1,0:T(8,128)(2,1)} %all-gather.3.cloned.1.call-done), kind=kOutput, calls=%fused_computation.38 | convolution fusion | flops 67215360 | bytes 1671168 | tf_op jit(solution)/shard_map/dot_general | solution.py:21
  70.0 0.0 copy-start.1
  70.0 3.2 %fusion = bf16[1,4096,256]{2,1,0:T(8,128)(2,1)} fusion(bf16[64,4096]{1,0:T(8,128)(2,1)} %copy-done.2, bf16[64,128]{1,0:T(8,128)(2,1)S(1)} %get-tuple-element.4, bf16[64,128]{1,0:T(8,128)(2,1)S(1)} %get-tuple-element.3), kind=kOutput, calls=%fused_computation.1 | convolution fusion | flops 135331840 | bytes 2654208 | tf_op jit(solution)/shard_map/dot_general | solution.py:74
  73.2 0.0 reduce-scatter.3.cloned.1.call-update
  73.3 0.0 copy-done.1
  73.3 1.6 %convolution_convert_fusion.2 = bf16[64,4096]{1,0:T(8,128)(2,1)} fusion(bf16[1,4096,256]{2,1,0:T(8,128)(2,1)S(1)} %copy-done.1, bf16[64,128]{1,0:T(8,128)(2,1)S(1)} %get-tuple-element.4, bf16[64,128]{1,0:T(8,128)(2,1)S(1)} %get-tuple-element.3), kind=kOutput, calls=%fused_computation.5 | convolution fusion | flops 134545408 | bytes 2654208 | tf_op jit(solution)/shard_map/dot_general | solution.py:80
  74.8 1.2 reshape.64
  76.1 19.9 %all_to_all.15 = bf16[16,4,4096]{2,1,0:T(4,128)(2,1)S(1)} all-to-all(bf16[16,4,4096]{2,1,0:T(4,128)(2,1)S(1)} %reshape.64), channel_id=1, replica_groups=mesh['dp'=2,'expert'=16] {'expert'}, dimensions={0} | all-to-all | bytes 1048576 | tf_op jit(solution)/shard_map/all_to_all | solution.py:91
  95.9 0.2 bitcast_reduce_fusion
  96.2 0.6 fusion.6
  96.8 1.5 %fusion.9 = bf16[128,4096]{1,0:T(8,128)(2,1)} fusion(f32[128,4096]{1,0:T(8,128)S(1)} %get-tuple-element.6, bf16[128,4096]{1,0:T(8,128)(2,1)S(1)} %copy-done, f32[128]{0:T(128)S(1)} %broadcast_multiply_fusion, f32[128]{0:T(128)S(1)} %add_rsqrt_fusion), kind=kLoop, calls=%fused_computation.17 | loop fusion | flops 3145728 | bytes 4195328 | tf_op jit(solution)/shard_map/convert_element_type | solution.py:106
  98.3 27.7 %reduce-scatter.3.cloned.1.call-done = bf16[1,2048,256]{2,1,0:T(8,128)(2,1)} async-done(((bf16[1,4096,256]{2,1,0:T(8,128)(2,1)}), bf16[1,2048,256]{2,1,0:T(8,128)(2,1)}) %reduce-scatter.3.cloned.1.call-update) | async-done | bytes 1048592 | tf_op jit(solution)/shard_map/reduce_scatter | solution.py:84
  (7 shorter events, 0.1 us)
Async XLA Ops:
  7.2 47.3 %all-gather.5.cloned.1.call-start = ((), (), s32[]{:S(2)}) async-start(), calls=%async_computation.6 | async-start | bytes 3145728 | tf_op jit(solution)/shard_map/all_gather | solution.py:60
  7.2 13.1 %copy-start = (bf16[128,4096]{1,0:T(8,128)(2,1)S(1)}, bf16[128,4096]{1,0:T(8,128)(2,1)}, u32[]{:S(2)}) copy-start(bf16[128,4096]{1,0:T(8,128)(2,1)} %param.7) | copy-start | bytes 3145732
  10.0 10.6 %copy-start.3 = (f32[4096]{0:T(1024)S(1)}, f32[4096]{0:T(1024)}, u32[]{:S(2)}) copy-start(f32[4096]{0:T(1024)} %param.11) | copy-start | bytes 49156
  12.9 21.8 %all-to-all-start = ((bf16[16,4,4096]{2,1,0:T(4,128)(2,1)}), bf16[16,4,4096]{2,1,0:T(4,128)(2,1)S(1)}, u32[]{:S(2)}, u32[]{:S(2)}) async-start(bf16[16,4,4096]{2,1,0:T(4,128)(2,1)} %bitcast), calls=%async_computation | async-start | bytes 1048576 | tf_op jit(solution)/shard_map/all_to_all | solution.py:69
  35.8 18.6 %all-to-all-start.1 = ((bf16[16,4,4096]{2,1,0:T(4,128)(2,1)}), bf16[16,4,4096]{2,1,0:T(4,128)(2,1)S(1)}, u32[]{:S(2)}, u32[]{:S(2)}) async-start(bf16[16,4,4096]{2,1,0:T(4,128)(2,1)} %bitcast.2), calls=%async_computation.1 | async-start | bytes 1048576 | tf_op jit(solution)/shard_map/all_to_all | solution.py:68
  39.9 28.4 %all-gather.3.cloned.1.call-start = ((), (), s32[]{:S(2)}) async-start(), calls=%async_computation.5 | async-start | bytes 1572864 | tf_op jit(solution)/shard_map/all_gather | solution.py:61
  40.6 57.7 %reduce-scatter.5.cloned.1.call-start = ((), (), s32[]{:S(2)}) async-start(), calls=%async_computation.8 | async-start | bytes 1572864 | tf_op jit(solution)/shard_map/reduce_scatter | solution.py:87
  54.4 3.8 %copy-start.2 = (bf16[64,4096]{1,0:T(8,128)(2,1)}, bf16[64,4096]{1,0:T(8,128)(2,1)S(1)}, u32[]{:S(2)}) copy-start(bf16[64,4096]{1,0:T(8,128)(2,1)S(1)} %reshape.63) | copy-start | bytes 1572868
  58.3 67.8 %reduce-scatter.3.cloned.1.call-start = ((), (), s32[]{:S(2)}) async-start(), calls=%async_computation.7 | async-start | bytes 3145728 | tf_op jit(solution)/shard_map/reduce_scatter | solution.py:84
  70.0 3.3 %copy-start.1 = (bf16[1,4096,256]{2,1,0:T(8,128)(2,1)S(1)}, bf16[1,4096,256]{2,1,0:T(8,128)(2,1)}, u32[]{:S(2)}) copy-start(bf16[1,4096,256]{2,1,0:T(8,128)(2,1)} %all-gather.5.cloned.1.call-done) | copy-start | bytes 6291460
Sparse Core Ops, SparseCore 0:
  9.5 35.8 all-gather.4
  46.9 21.2 all-gather.2
  71.1 20.3 reduce-scatter.4
  94.2 31.8 reduce-scatter.2
where the time goes:
time: 133 us
  waiting for transfers between devices  66.4 us (50%)
  blocking collectives  19.9 us (15%)
  between operations  13.9 us (10%)
  matrix products  12.8 us (10%)
  starting transfers between devices  11.6 us (9%)
  local copies, waits for them, and re-layouts  5.16 us (4%)
  other arithmetic  2.83 us (2%)
    reduce_scatter x1, waiting for transfers between devices, body(): lax.psum_scatter(part_gu[None].astype(jnp.bfloat16), 'dp', scatter_dimens...  27.7 us
    all_to_all x1, blocking collectives, body(): lax.all_to_all(back.reshape(members, CAP, width), 'expert', split_axis=0,...  19.9 us
    all_to_all x1, waiting for transfers between devices, body(): lax.all_to_all(wide_dy, 'expert', split_axis=0, concat_axis=0, tiled=True)  13.7 us
    all_to_all x1, waiting for transfers between devices, body(): lax.all_to_all(wide_in, 'expert', split_axis=0, concat_axis=0, tiled=True)  13.5 us
    all_gather x1, waiting for transfers between devices, body(): lax.all_gather(w_down, 'dp', axis=2, tiled=True)  9.97 us
    all_to_all x1, starting transfers between devices, body(): lax.all_to_all(wide_dy, 'expert', split_axis=0, concat_axis=0, tiled=True)  7.36 us
    all_to_all x1, starting transfers between devices, body(): lax.all_to_all(wide_in, 'expert', split_axis=0, concat_axis=0, tiled=True)  4.1 us
    dot_general x1, matrix products, body(): lax.dot_general(rows_in, d_pre, (((0,), (0,)), ((), ())), preferred_eleme...  3.23 us
  transfers between devices with their start and end apart: 6, of which 4 were waited for; matrix products, arithmetic and copies ran while one was open for 16% of the time, Pallas kernels for 0%

commit v1 on v0

v1 whole, which is shorter than its diff:
```python
import functools

import jax
import jax.numpy as jnp
from jax import lax
from jax.experimental import pallas as pl
from jax.experimental.pallas import tpu as pltpu
from jax.sharding import PartitionSpec as P

SLICES = 8
CAP = 4
EPS = 1e-06
F32 = jnp.float32
BF = jnp.bfloat16


def kernel(n_dp, groups, lat, dout, routes, gate_w, gain, wgu, wd, out_lat, out_gu, out_d,
           inrow, dyrow, sendbuf, stage, gath, xs, ys, part, xr, bk, rb1, rb2, acc, mid, homest, homeb, fin, table,
           s1, r1, s2, r2, s3, r3, sx, rx, s4, r4, s5, r5, s6, r6):
    patches, width = lat.shape
    dw = width // n_dp
    half = dw // 2
    quarter = dw // 4
    slots = n_dp * groups
    nr = groups * CAP
    hid = wd.shape[1]
    d = lax.axis_index("dp")
    j = lax.axis_index("expert")
    hi = j // SLICES
    m = j % SLICES
    bit0 = m % 2
    bit1 = (m // 2) % 2
    bit2 = m // 4
    f0 = 1 - 2 * bit0
    f1 = 2 - 4 * bit1
    f2 = 4 - 8 * bit2
    planes = (m + f1, m + f2, m + f1 + f2)
    ms = d * groups + hi

    def dev(dd, jj):
        return {"dp": dd, "expert": jj}

    def slot_dev(t):
        p = (ms + t) % slots
        return p, dev(p // groups, (p % groups) * SLICES + m)

    def rcopy(src, dst, ss, rs, to):
        return pltpu.make_async_remote_copy(
            src_ref=src, dst_ref=dst, send_sem=ss, recv_sem=rs, device_id=to,
            device_id_type=pl.DeviceIdType.MESH)

    sib = dev(d, hi * SLICES + m + f0)
    plane_devs = [dev(d, hi * SLICES + q) for q in planes]
    barrier = pltpu.get_barrier_semaphore()
    for t in range(1, slots):
        pl.semaphore_signal(barrier, inc=1, device_id=slot_dev(t)[1], device_id_type=pl.DeviceIdType.MESH)
    for to in [sib] + plane_devs:
        pl.semaphore_signal(barrier, inc=1, device_id=to, device_id_type=pl.DeviceIdType.MESH)

    r = routes[...]
    g = gate_w[...]
    c0, c1 = r[:, 0:1], r[:, 1:2]
    in0, in1 = c0 < groups, c1 < groups
    chosen = jnp.where(in0, c0, jnp.where(in1, c1, -1)).astype(F32)
    weight = jnp.where(in0, g[:, 0:1], 0.0) + jnp.where(in1, g[:, 1:2], 0.0)
    lane = lax.broadcasted_iota(jnp.int32, (patches, 128), 1).astype(F32)
    onehot = jnp.where(chosen == lane, 1.0, 0.0)
    low = (lax.broadcasted_iota(jnp.int32, (patches, patches), 1)
           < lax.broadcasted_iota(jnp.int32, (patches, patches), 0))
    prefix = jnp.dot(jnp.where(low, 1.0, 0.0).astype(BF), onehot.astype(BF), preferred_element_type=F32)
    slot = jnp.sum(prefix * onehot, axis=1, keepdims=True)
    target = jnp.where(chosen >= 0.0, chosen * CAP + slot, -1.0)
    sel_t = jnp.where(target == lane, 1.0, 0.0)
    sel = sel_t.T
    w_rows = jnp.sum((sel_t * weight).T, axis=1, keepdims=True)[:nr]
    pick = sel[:nr].astype(BF)
    raw = jnp.dot(pick, lat[...], preferred_element_type=F32)
    inverse = lax.rsqrt(jnp.mean(raw * raw, axis=1, keepdims=True) + EPS)
    scaled = raw * inverse
    inrow[...] = scaled * gain[...]
    dyrow[...] = w_rows * jnp.dot(pick, dout[...], preferred_element_type=F32)
    for dd in range(n_dp):
        for e in range(groups):
            for k in range(4):
                src = inrow if k < 2 else dyrow
                lo = dd * dw + (k % 2) * half
                stage[CAP * k:CAP * (k + 1), :] = src[CAP * e:CAP * (e + 1), lo:lo + half]
            sendbuf[dd * groups + e] = stage[...].astype(BF)

    pl.semaphore_wait(barrier, slots + 3)
    first = []
    for t in range(1, slots):
        p, to = slot_dev(t)
        c = rcopy(sendbuf.at[p], gath.at[m, ms], s1.at[t], r1.at[t], to)
        c.start()
        first.append(c)
    gath[m, ms] = sendbuf[ms]
    for c in first:
        c.wait()
    sends = []
    for i in range(3):
        c = rcopy(gath.at[m], gath.at[m], s2.at[i], r2.at[i], plane_devs[i])
        c.start()
        sends.append(c)
    own = rcopy(gath.at[m], gath.at[m], s3.at[3], r3.at[3], sib)
    own.start()
    relay = [own]
    for i in range(3):
        sends[i].wait_recv()
        c = rcopy(gath.at[planes[i]], gath.at[planes[i]], s3.at[i], r3.at[i], sib)
        c.start()
        relay.append(c)
    for c in relay:
        c.wait_recv()

    row = lax.broadcasted_iota(jnp.int32, (64, 64), 0)
    col = lax.broadcasted_iota(jnp.int32, (64, 64), 1)
    perm = jnp.where(col == ((row // 4) % 4) * 16 + (row // 16) * 4 + row % 4, 1.0, 0.0).astype(BF)
    per = slots // 4

    def arrange(c, carry):
        block = gath[c // per, pl.ds((c % per) * 4, 4)].reshape(64, half)
        s = jnp.dot(perm, block, preferred_element_type=F32).astype(BF)
        at = pl.ds(pl.multiple_of(c * 16, 16), 16)
        xs[at, :half] = s[:16]
        xs[at, half:] = s[16:32]
        ys[at, :half] = s[32:48]
        ys[at, half:] = s[48:]
        return carry

    lax.fori_loop(0, SLICES * per, arrange, 0)
    part[:, :2 * hid] = jnp.dot(xs[...], wgu[0], preferred_element_type=F32)
    part[:, 2 * hid:] = lax.dot_general(ys[...], wd[0], (((1,), (1,)), ((), ())), preferred_element_type=F32)
    xch = []
    for t in range(1, n_dp):
        c = rcopy(part, xr.at[t - 1], sx.at[t - 1], rx.at[t - 1], dev((d + t) % n_dp, j))
        c.start()
        xch.append(c)
    for c in sends + relay:
        c.wait_send()
    total = part[...]
    for t in range(1, n_dp):
        xch[t - 1].wait_recv()
        total = total + xr[t - 1]
    gate, up, dh = total[:, :hid], total[:, hid:2 * hid], total[:, 2 * hid:]
    sig = jax.nn.sigmoid(gate)
    act = gate * sig
    hidden = (act * up).astype(BF)
    d_gate = dh * up * sig * (1.0 + gate * (1.0 - sig))
    d_pre = jnp.concatenate([d_gate, dh * act], axis=1).astype(BF)
    rows_m = slots * CAP
    bk[...] = lax.dot_general(d_pre, wgu[0], (((1,), (1,)), ((), ())),
                              preferred_element_type=F32).astype(BF).reshape(SLICES, rows_m, dw)
    mine = planes + (m,)
    to_sib = []
    for i in range(4):
        c = rcopy(bk.at[mine[i] + f0], rb1.at[i], s4.at[i], r4.at[i], sib)
        c.start()
        to_sib.append(c)
    over = lax.dot_general(xs[...], d_pre, (((0,), (0,)), ((), ())), preferred_element_type=F32)
    out_gu[0] = over.astype(BF)
    to_plane = []
    for i in range(4):
        to_sib[i].wait_recv()
        both = bk[mine[i]].astype(F32) + rb1[i].astype(F32)
        if i < 3:
            mid[i] = both.astype(BF)
            c = rcopy(mid.at[i], rb2.at[i], s5.at[i], r5.at[i], plane_devs[i])
            c.start()
            to_plane.append(c)
        else:
            acc[...] = both
    out_d[0] = lax.dot_general(hidden, ys[...], (((0,), (0,)), ((), ())), preferred_element_type=F32).astype(BF)
    for i in range(3):
        to_plane[i].wait_recv()
        acc[...] += rb2[i].astype(F32)
    for s in range(slots):
        for q in range(4):
            homest[CAP * q:CAP * (q + 1), :] = acc[CAP * s:CAP * (s + 1), q * quarter:(q + 1) * quarter]
        homeb[s] = homest[...].astype(BF)
    home = []
    for t in range(1, slots):
        p, to = slot_dev(t)
        c = rcopy(homeb.at[p], fin.at[ms], s6.at[t], r6.at[t], to)
        c.start()
        home.append(c)
    fin[ms] = homeb[ms]
    for c in xch + to_sib + to_plane:
        c.wait_send()
    for c in home:
        c.wait()
    for dd in range(n_dp):
        for e in range(groups):
            homest[...] = fin[dd * groups + e].astype(F32)
            for q in range(4):
                lo = dd * dw + q * quarter
                table[CAP * e:CAP * (e + 1), lo:lo + quarter] = homest[CAP * q:CAP * (q + 1), :]
    grad_in = table[...] * gain[...]
    d_rows = inverse * (grad_in - scaled * jnp.mean(grad_in * scaled, axis=1, keepdims=True))
    put = sel[:nr].astype(BF)
    out_lat[...] = lax.dot_general(put, d_rows.astype(BF), (((0,), (0,)), ((), ())),
                                   preferred_element_type=F32).astype(BF)


def body(latent, dout, routes, gate_w, norm_gain, w_gate_up, w_down):
    patches, width = latent.shape
    n_dp = lax.axis_size("dp")
    groups = lax.axis_size("expert") // SLICES
    slots = n_dp * groups
    nr = groups * CAP
    dw = width // n_dp
    hid = w_down.shape[1]
    rows = SLICES * slots * CAP
    rows_m = slots * CAP
    vm = pltpu.VMEM
    dma = pltpu.SemaphoreType.DMA
    pairs = []
    for n in (slots, 3, 4, max(n_dp - 1, 1), 4, 3, slots):
        pairs += [dma((n,)), dma((n,))]
    return pl.pallas_call(
        functools.partial(kernel, n_dp, groups),
        out_shape=(
            jax.ShapeDtypeStruct(latent.shape, BF),
            jax.ShapeDtypeStruct(w_gate_up.shape, BF),
            jax.ShapeDtypeStruct(w_down.shape, BF),
        ),
        in_specs=[pl.BlockSpec(memory_space=vm)] * 7,
        out_specs=(pl.BlockSpec(memory_space=vm),) * 3,
        scratch_shapes=[
            vm((nr, width), F32), vm((nr, width), F32),
            vm((slots, 16, dw // 2), BF), vm((16, dw // 2), F32),
            vm((SLICES, slots, 16, dw // 2), BF),
            vm((rows, dw), BF), vm((rows, dw), BF),
            vm((rows, 3 * hid), F32), vm((max(n_dp - 1, 1), rows, 3 * hid), F32),
            vm((SLICES, rows_m, dw), BF), vm((4, rows_m, dw), BF), vm((3, rows_m, dw), BF),
            vm((rows_m, dw), F32), vm((3, rows_m, dw), BF),
            vm((16, dw // 4), F32), vm((slots, 16, dw // 4), BF), vm((slots, 16, dw // 4), BF),
            vm((nr, width), F32),
        ] + pairs,
        compiler_params=pltpu.CompilerParams(
            collective_id=0, has_side_effects=True, vmem_limit_bytes=60 * 1024 * 1024),
    )(latent, dout, routes, gate_w, norm_gain.reshape(1, width), w_gate_up, w_down)


def solution(mesh):
    placed = (
        P(("dp", "expert"), None),
        P(("dp", "expert"), None),
        P(("dp", "expert"), None),
        P(("dp", "expert"), None),
        P(),
        P("expert", "dp", None),
        P("expert", None, "dp"),
    )
    return jax.shard_map(
        body,
        mesh=mesh,
        in_specs=placed,
        out_specs=(P(("dp", "expert"), None), P("expert", "dp", None), P("expert", None, "dp")),
        check_vma=False,
    )
```

time: 133 us -> 48.7 us (0.37)
  waiting for transfers between devices: 66.4 us -> 0 us
  Pallas kernels: 0 us -> 41.1 us
  blocking collectives: 19.9 us -> 0 us
  between operations: 13.9 us -> 0.66 us
  matrix products: 12.8 us -> 0 us
  starting transfers between devices: 11.6 us -> 0 us
  other arithmetic: 2.83 us -> 0 us
  local copies, waits for them, and re-layouts: 5.16 us -> 6.72 us
    pallas_call x0 -> x1, Pallas kernels: none -> 41.1 us  [body(): pl.pallas_call(functools.partial(kernel, n_dp, groups), out_shape=(jax.Sh...]
    reduce_scatter x2 -> x0, waiting for transfers between devices: 27.8 us -> none  [the longest x1 27.7 us: body(): lax.psum_scatter(part_gu[None].astype(jnp.bfloat16), 'dp', scatter_dimens...]
    all_to_all x2 -> x0, waiting for transfers between devices: 27.2 us -> none  [the longest x1 13.7 us: body(): lax.all_to_all(wide_dy, 'expert', split_axis=0, concat_axis=0, tiled=True)]
    all_to_all x1 -> x0, blocking collectives: 19.9 us -> none  [body(): lax.all_to_all(back.reshape(members, CAP, width), 'expert', split_axis=0,...]
    dot_general x8 -> x0, matrix products: 12.8 us -> none  [the longest x1 3.23 us: body(): lax.dot_general(rows_in, d_pre, (((0,), (0,)), ((), ())), preferred_eleme...]
    all_to_all x2 -> x0, starting transfers between devices: 11.5 us -> none  [the longest x1 7.36 us: body(): lax.all_to_all(wide_dy, 'expert', split_axis=0, concat_axis=0, tiled=True)]
    all_gather x2 -> x0, waiting for transfers between devices: 9.99 us -> none  [the longest x1 9.97 us: body(): lax.all_gather(w_down, 'dp', axis=2, tiled=True)]
    unnamed x10 -> x13, local copies, waits for them, and re-layouts: 1.59 us -> 6.72 us
  transfers between devices with their start and end apart: 6 -> 0, of which waited for: 4 -> 0; matrix products, arithmetic and copies ran while one was open for 16% -> 0% of each run, Pallas kernels for 0% -> 0%
where the time goes in v1:
time: 48.7 us; the launch traced here: 48.5 us
  Pallas kernels  41.1 us (84%)
  local copies, waits for them, and re-layouts  6.72 us (14%)
  between operations  0.66 us (1%)
    pallas_call x1, Pallas kernels, body(): pl.pallas_call(functools.partial(kernel, n_dp, groups), out_shape=(jax.Sh...  41.1 us
    unnamed x13, local copies, waits for them, and re-layouts  6.72 us

profile of v1, /device:TPU:0, one launch (start us, length us, event | category | flops | bytes accessed | tf_op | source)
XLA Modules:
  0.0 48.5 jit_solution(4576085035397123351)
XLA Ops:
  0.6 0.0 copy-start.2
  0.6 0.7 %copy-done.2 = s32[128,2]{0,1:T(2,128)S(1)} copy-done((s32[128,2]{0,1:T(2,128)S(1)}, s32[128,2]{0,1:T(2,128)}, u32[]{:S(2)}) %copy-start.2) | copy-done | bytes 1048
  1.3 0.0 copy-start.3
  1.3 0.7 %copy.10.routes = s32[128,2]{1,0:T(8,128)} copy(s32[128,2]{0,1:T(2,128)S(1)} %copy-done.2) | data formatting | bytes 2048 | tf_op args[2]
  2.1 0.0 copy-done.3
  2.1 0.7 %copy.11.gate_w = f32[128,2]{1,0:T(8,128)} copy(f32[128,2]{0,1:T(2,128)S(1)} %copy-done.3) | data formatting | bytes 2048 | tf_op args[3]
  2.8 41.1 %shard_map.94 = (bf16[128,4096]{1,0:T(8,128)(2,1)}, bf16[1,2048,256]{2,1,0:T(8,128)(2,1)}, bf16[1,128,2048]{2,1,0:T(8,128)(2,1)}) custom-call(bf16[128,4096]{1,0:T(8,128)(2,1)} %lat.1, bf16[128,4096]{1,0:T(8,128)(2,1)} %dout.1, s32[128,2]{1,0:T(8,128)} %copy.10.routes, f32[128,2]{1,0:T(8,128)} %copy.11.gate_w, f32[1,4096]{1,0:T(1,128)} %bitcast.1, ...), custom_call_target="tpu_custom_call" | custom-call | tf_op jit(solution)/shard_map/pallas_call | solution.py:220
  43.9 0.0 copy-start
  43.9 2.4 %copy.15 = bf16[128,4096]{1,0:T(8,128)(2,1)} copy(bf16[128,4096]{1,0:T(8,128)(2,1)} %get-tuple-element.6) | data formatting | bytes 2097152
  46.3 0.0 copy-done
  46.3 0.0 copy-start.1
  46.3 1.0 %copy.16 = bf16[1,2048,256]{2,1,0:T(8,128)(2,1)} copy(bf16[1,2048,256]{2,1,0:T(8,128)(2,1)S(1)} %copy-done) | data formatting | bytes 2097152
  47.3 0.4 copy-done.1
  47.7 0.8 %copy.17 = bf16[1,128,2048]{2,1,0:T(8,128)(2,1)} copy(bf16[1,128,2048]{2,1,0:T(8,128)(2,1)S(1)} %copy-done.1) | data formatting | bytes 1048576
Async XLA Ops:
  0.6 0.7 %copy-start.2 = (s32[128,2]{0,1:T(2,128)S(1)}, s32[128,2]{0,1:T(2,128)}, u32[]{:S(2)}) copy-start(s32[128,2]{0,1:T(2,128)} %param.9) | copy-start | bytes 3076
  1.3 0.7 %copy-start.3 = (f32[128,2]{0,1:T(2,128)S(1)}, f32[128,2]{0,1:T(2,128)}, u32[]{:S(2)}) copy-start(f32[128,2]{0,1:T(2,128)} %param.10) | copy-start | bytes 3076
  43.9 2.4 %copy-start = (bf16[1,2048,256]{2,1,0:T(8,128)(2,1)S(1)}, bf16[1,2048,256]{2,1,0:T(8,128)(2,1)}, u32[]{:S(2)}) copy-start(bf16[1,2048,256]{2,1,0:T(8,128)(2,1)} %get-tuple-element.7) | copy-start | bytes 3145732
  46.3 1.4 %copy-start.1 = (bf16[1,128,2048]{2,1,0:T(8,128)(2,1)S(1)}, bf16[1,128,2048]{2,1,0:T(8,128)(2,1)}, u32[]{:S(2)}) copy-start(bf16[1,128,2048]{2,1,0:T(8,128)(2,1)} %get-tuple-element.8) | copy-start | bytes 1572868

commit v2 on v1

--- a/solution.py
+++ b/solution.py
@@ -14,10 +14,10 @@
 BF = jnp.bfloat16
 
 
-def kernel(n_dp, groups, lat, dout, routes, gate_w, gain, wgu, wd, out_lat, out_gu, out_d,
-           inrow, dyrow, sendbuf, stage, gath, xs, ys, part, xr, bk, rb1, rb2, acc, mid, homest, homeb, fin, table,
+def kernel(n_dp, groups, lat_h, dout_h, routes, gate_w, gain, wgu_h, wd_h, out_rows, out_sel, out_gu, out_d,
+           lat, dout, wgu, wd, ld, inrow, dyrow, sendbuf, stage, gath, xs, ys, part, xr, bk, rb1, rb2, acc, mid, homest, homeb, fin, table,
            s1, r1, s2, r2, s3, r3, sx, rx, s4, r4, s5, r5, s6, r6):
-    patches, width = lat.shape
+    patches, width = lat_h.shape
     dw = width // n_dp
     half = dw // 2
     quarter = dw // 4
@@ -57,23 +57,30 @@
     for to in [sib] + plane_devs:
         pl.semaphore_signal(barrier, inc=1, device_id=to, device_id_type=pl.DeviceIdType.MESH)
 
+    loads = []
+    for i, (a, b) in enumerate(((lat_h, lat), (dout_h, dout), (wgu_h, wgu), (wd_h, wd))):
+        c = pltpu.make_async_copy(a, b, ld.at[i])
+        c.start()
+        loads.append(c)
     r = routes[...]
     g = gate_w[...]
-    c0, c1 = r[:, 0:1], r[:, 1:2]
+    c0, c1 = r[0:1, :], r[1:2, :]
     in0, in1 = c0 < groups, c1 < groups
     chosen = jnp.where(in0, c0, jnp.where(in1, c1, -1)).astype(F32)
-    weight = jnp.where(in0, g[:, 0:1], 0.0) + jnp.where(in1, g[:, 1:2], 0.0)
-    lane = lax.broadcasted_iota(jnp.int32, (patches, 128), 1).astype(F32)
-    onehot = jnp.where(chosen == lane, 1.0, 0.0)
-    low = (lax.broadcasted_iota(jnp.int32, (patches, patches), 1)
-           < lax.broadcasted_iota(jnp.int32, (patches, patches), 0))
-    prefix = jnp.dot(jnp.where(low, 1.0, 0.0).astype(BF), onehot.astype(BF), preferred_element_type=F32)
-    slot = jnp.sum(prefix * onehot, axis=1, keepdims=True)
+    weight = jnp.where(in0, g[0:1, :], 0.0) + jnp.where(in1, g[1:2, :], 0.0)
+    place = lax.broadcasted_iota(jnp.int32, (128, patches), 0).astype(F32)
+    onehot = jnp.where(chosen == place, 1.0, 0.0)
+    before = (lax.broadcasted_iota(jnp.int32, (patches, patches), 0)
+              < lax.broadcasted_iota(jnp.int32, (patches, patches), 1))
+    prefix = jnp.dot(onehot.astype(BF), jnp.where(before, 1.0, 0.0).astype(BF), preferred_element_type=F32)
+    slot = jnp.sum(prefix * onehot, axis=0, keepdims=True)
     target = jnp.where(chosen >= 0.0, chosen * CAP + slot, -1.0)
-    sel_t = jnp.where(target == lane, 1.0, 0.0)
-    sel = sel_t.T
-    w_rows = jnp.sum((sel_t * weight).T, axis=1, keepdims=True)[:nr]
-    pick = sel[:nr].astype(BF)
+    sel = jnp.where(target == place, 1.0, 0.0)[:nr]
+    out_sel[...] = sel
+    w_rows = jnp.sum(sel * weight, axis=1, keepdims=True)
+    pick = sel.astype(BF)
+    loads[0].wait()
+    loads[1].wait()
     raw = jnp.dot(pick, lat[...], preferred_element_type=F32)
     inverse = lax.rsqrt(jnp.mean(raw * raw, axis=1, keepdims=True) + EPS)
     scaled = raw * inverse
@@ -95,24 +102,19 @@
         c.start()
         first.append(c)
     gath[m, ms] = sendbuf[ms]
-    for c in first:
-        c.wait()
+    order = [t for t in range(slots) if t % groups == 0] + [t for t in range(slots) if t % groups]
     sends = []
-    for i in range(3):
-        c = rcopy(gath.at[m], gath.at[m], s2.at[i], r2.at[i], plane_devs[i])
-        c.start()
-        sends.append(c)
+    for t in order:
+        at = (ms + slots - t) % slots
+        if t:
+            first[t - 1].wait_recv()
+        for i in range(3):
+            c = rcopy(gath.at[m, at], gath.at[m, at], s2.at[i * slots + t], r2.at[i * slots + t], plane_devs[i])
+            c.start()
+            sends.append((i, c))
     own = rcopy(gath.at[m], gath.at[m], s3.at[3], r3.at[3], sib)
     own.start()
     relay = [own]
-    for i in range(3):
-        sends[i].wait_recv()
-        c = rcopy(gath.at[planes[i]], gath.at[planes[i]], s3.at[i], r3.at[i], sib)
-        c.start()
-        relay.append(c)
-    for c in relay:
-        c.wait_recv()
-
     row = lax.broadcasted_iota(jnp.int32, (64, 64), 0)
     col = lax.broadcasted_iota(jnp.int32, (64, 64), 1)
     perm = jnp.where(col == ((row // 4) % 4) * 16 + (row // 16) * 4 + row % 4, 1.0, 0.0).astype(BF)
@@ -128,20 +130,38 @@
         ys[at, half:] = s[48:]
         return carry
 
-    lax.fori_loop(0, SLICES * per, arrange, 0)
-    part[:, :2 * hid] = jnp.dot(xs[...], wgu[0], preferred_element_type=F32)
-    part[:, 2 * hid:] = lax.dot_general(ys[...], wd[0], (((1,), (1,)), ((), ())), preferred_element_type=F32)
+    pair_rows = 2 * slots * CAP
     xch = []
+    for n in range(4):
+        if n:
+            for i, c in sends:
+                if i == n - 1:
+                    c.wait_recv()
+            c = rcopy(gath.at[planes[n - 1]], gath.at[planes[n - 1]], s3.at[n - 1], r3.at[n - 1], sib)
+            c.start()
+            relay.append(c)
+        relay[n].wait_recv()
+        pair = (planes[n - 1] if n else m) // 2
+        lax.fori_loop(pair * 2 * per, pair * 2 * per + 2 * per, arrange, 0)
+        if n == 0:
+            loads[2].wait()
+            loads[3].wait()
+        at = pl.ds(pl.multiple_of(pair * pair_rows, 16), pair_rows)
+        part[pair, :, :2 * hid] = jnp.dot(xs[at, :], wgu[0], preferred_element_type=F32)
+        part[pair, :, 2 * hid:] = lax.dot_general(ys[at, :], wd[0], (((1,), (1,)), ((), ())),
+                                                  preferred_element_type=F32)
+        for t in range(1, n_dp):
+            k = (t - 1) * 4 + n
+            c = rcopy(part.at[pair], xr.at[t - 1, pair], sx.at[k], rx.at[k], dev((d + t) % n_dp, j))
+            c.start()
+            xch.append(c)
+    for c in first + [c for _, c in sends] + relay:
+        c.wait_send()
+    for c in xch:
+        c.wait_recv()
+    total = part[...].reshape(4 * pair_rows, 3 * hid)
     for t in range(1, n_dp):
-        c = rcopy(part, xr.at[t - 1], sx.at[t - 1], rx.at[t - 1], dev((d + t) % n_dp, j))
-        c.start()
-        xch.append(c)
-    for c in sends + relay:
-        c.wait_send()
-    total = part[...]
-    for t in range(1, n_dp):
-        xch[t - 1].wait_recv()
-        total = total + xr[t - 1]
+        total = total + xr[t - 1].reshape(4 * pair_rows, 3 * hid)
     gate, up, dh = total[:, :hid], total[:, hid:2 * hid], total[:, 2 * hid:]
     sig = jax.nn.sigmoid(gate)
     act = gate * sig
@@ -197,9 +217,18 @@
                 table[CAP * e:CAP * (e + 1), lo:lo + quarter] = homest[CAP * q:CAP * (q + 1), :]
     grad_in = table[...] * gain[...]
     d_rows = inverse * (grad_in - scaled * jnp.mean(grad_in * scaled, axis=1, keepdims=True))
-    put = sel[:nr].astype(BF)
-    out_lat[...] = lax.dot_general(put, d_rows.astype(BF), (((0,), (0,)), ((), ())),
+    out_rows[...] = d_rows
+
+
+def finish(rows, sel, gu, dn, out_lat, out_gu, out_d, sem):
+    a = pltpu.make_async_copy(gu, out_gu, sem.at[0])
+    b = pltpu.make_async_copy(dn, out_d, sem.at[1])
+    a.start()
+    b.start()
+    out_lat[...] = lax.dot_general(sel[...].astype(BF), rows[...].astype(BF), (((0,), (0,)), ((), ())),
                                    preferred_element_type=F32).astype(BF)
+    a.wait()
+    b.wait()
 
 
 def body(latent, dout, routes, gate_w, norm_gain, w_gate_up, w_down):
@@ -215,23 +244,27 @@
     vm = pltpu.VMEM
     dma = pltpu.SemaphoreType.DMA
     pairs = []
-    for n in (slots, 3, 4, max(n_dp - 1, 1), 4, 3, slots):
+    for n in (slots, 3 * slots, 4, 4 * max(n_dp - 1, 1), 4, 3, slots):
         pairs += [dma((n,)), dma((n,))]
-    return pl.pallas_call(
+    any_ = pl.BlockSpec(memory_space=pl.ANY)
+    vms = pl.BlockSpec(memory_space=vm)
+    d_rows, sel, gu, dn = pl.pallas_call(
         functools.partial(kernel, n_dp, groups),
         out_shape=(
-            jax.ShapeDtypeStruct(latent.shape, BF),
+            jax.ShapeDtypeStruct((nr, width), F32),
+            jax.ShapeDtypeStruct((nr, patches), F32),
             jax.ShapeDtypeStruct(w_gate_up.shape, BF),
             jax.ShapeDtypeStruct(w_down.shape, BF),
         ),
-        in_specs=[pl.BlockSpec(memory_space=vm)] * 7,
-        out_specs=(pl.BlockSpec(memory_space=vm),) * 3,
+        in_specs=[any_, any_, vms, vms, vms, any_, any_],
+        out_specs=(vms,) * 4,
         scratch_shapes=[
+            vm(latent.shape, BF), vm(dout.shape, BF), vm(w_gate_up.shape, BF), vm(w_down.shape, BF), dma((4,)),
             vm((nr, width), F32), vm((nr, width), F32),
             vm((slots, 16, dw // 2), BF), vm((16, dw // 2), F32),
             vm((SLICES, slots, 16, dw // 2), BF),
             vm((rows, dw), BF), vm((rows, dw), BF),
-            vm((rows, 3 * hid), F32), vm((max(n_dp - 1, 1), rows, 3 * hid), F32),
+            vm((4, rows // 4, 3 * hid), F32), vm((max(n_dp - 1, 1), 4, rows // 4, 3 * hid), F32),
             vm((SLICES, rows_m, dw), BF), vm((4, rows_m, dw), BF), vm((3, rows_m, dw), BF),
             vm((rows_m, dw), F32), vm((3, rows_m, dw), BF),
             vm((16, dw // 4), F32), vm((slots, 16, dw // 4), BF), vm((slots, 16, dw // 4), BF),
@@ -239,7 +272,19 @@
         ] + pairs,
         compiler_params=pltpu.CompilerParams(
             collective_id=0, has_side_effects=True, vmem_limit_bytes=60 * 1024 * 1024),
-    )(latent, dout, routes, gate_w, norm_gain.reshape(1, width), w_gate_up, w_down)
+    )(latent, dout, routes.T, gate_w.T, norm_gain.reshape(1, width), w_gate_up, w_down)
+    return pl.pallas_call(
+        finish,
+        out_shape=(
+            jax.ShapeDtypeStruct(latent.shape, BF),
+            jax.ShapeDtypeStruct(w_gate_up.shape, BF),
+            jax.ShapeDtypeStruct(w_down.shape, BF),
+        ),
+        in_specs=[vms, vms, any_, any_],
+        out_specs=(vms, any_, any_),
+        scratch_shapes=[dma((2,))],
+        compiler_params=pltpu.CompilerParams(vmem_limit_bytes=60 * 1024 * 1024),
+    )(d_rows, sel, gu, dn)
 
 
 def solution(mesh):

time: 48.7 us -> 86.5 us (1.78)
  Pallas kernels: 41.1 us -> 85.6 us
  local copies, waits for them, and re-layouts: 6.72 us -> 0 us
    pallas_call x0 -> x1, Pallas kernels: none -> 50.6 us  [body(): pl.pallas_call(finish, out_shape=(jax.ShapeDtypeStruct(latent.shape, BF),...]
    unnamed x13 -> x0, local copies, waits for them, and re-layouts: 6.72 us -> none
    pallas_call x1, Pallas kernels: 41.1 us -> 35 us  [body(): pl.pallas_call(functools.partial(kernel, n_dp, groups), out_shape=(jax.Sh...]
where the time goes in v2:
time: 86.5 us; the launch traced here: 86.3 us
  Pallas kernels  85.6 us (99%)
    pallas_call x1, Pallas kernels, body(): pl.pallas_call(finish, out_shape=(jax.ShapeDtypeStruct(latent.shape, BF),...  50.6 us
    pallas_call x1, Pallas kernels, body(): pl.pallas_call(functools.partial(kernel, n_dp, groups), out_shape=(jax.Sh...  35 us

profile of v2, /device:TPU:0, one launch (start us, length us, event | category | flops | bytes accessed | tf_op | source)
XLA Modules:
  0.0 86.3 jit_solution(655553709890985654)
XLA Ops:
  0.6 35.0 %shard_map.94 = (f32[8,4096]{1,0:T(8,128)}, f32[8,128]{1,0:T(8,128)}, bf16[1,2048,256]{2,1,0:T(8,128)(2,1)}, bf16[1,128,2048]{2,1,0:T(8,128)(2,1)}) custom-call(bf16[128,4096]{1,0:T(8,128)(2,1)} %lat_h.1, bf16[128,4096]{1,0:T(8,128)(2,1)} %dout_h.1, s32[2,128]{1,0:T(2,128)} %bitcast.4, f32[2,128]{1,0:T(2,128)} %bitcast.5, f32[1,4096]{1,0:T(1,128)} %bitcast.3, ...), custom_call_target="tpu_custom_call" | custom-call | tf_op jit(solution)/shard_map/pallas_call | solution.py:251
  35.6 50.6 %shard_map.95 = (bf16[128,4096]{1,0:T(8,128)(2,1)}, bf16[1,2048,256]{2,1,0:T(8,128)(2,1)}, bf16[1,128,2048]{2,1,0:T(8,128)(2,1)}) custom-call(f32[8,4096]{1,0:T(8,128)} %get-tuple-element.7.rows, f32[8,128]{1,0:T(8,128)} %get-tuple-element.8.sel, bf16[1,2048,256]{2,1,0:T(8,128)(2,1)} %get-tuple-element.9.gu, bf16[1,128,2048]{2,1,0:T(8,128)(2,1)} %get-tuple-element.10.dn), custom_call_target="tpu_custom_call" | custom-call | tf_op jit(solution)/shard_map/pallas_call | solution.py:276

commit v3 on v2

--- a/solution.py
+++ b/solution.py
@@ -15,7 +15,7 @@
 
 
 def kernel(n_dp, groups, lat_h, dout_h, routes, gate_w, gain, wgu_h, wd_h, out_rows, out_sel, out_gu, out_d,
-           lat, dout, wgu, wd, ld, inrow, dyrow, sendbuf, stage, gath, xs, ys, part, xr, bk, rb1, rb2, acc, mid, homest, homeb, fin, table,
+           lat, dout, wgu, wd, gus, dns, ld, inrow, dyrow, sendbuf, stage, gath, xs, ys, part, xr, bk, rb1, rb2, acc, mid, homest, homeb, fin, table,
            s1, r1, s2, r2, s3, r3, sx, rx, s4, r4, s5, r5, s6, r6):
     patches, width = lat_h.shape
     dw = width // n_dp
@@ -177,8 +177,9 @@
         c = rcopy(bk.at[mine[i] + f0], rb1.at[i], s4.at[i], r4.at[i], sib)
         c.start()
         to_sib.append(c)
-    over = lax.dot_general(xs[...], d_pre, (((0,), (0,)), ((), ())), preferred_element_type=F32)
-    out_gu[0] = over.astype(BF)
+    dns[0] = lax.dot_general(hidden, ys[...], (((0,), (0,)), ((), ())), preferred_element_type=F32).astype(BF)
+    w_d = pltpu.make_async_copy(dns, out_d, ld.at[4])
+    w_d.start()
     to_plane = []
     for i in range(4):
         to_sib[i].wait_recv()
@@ -190,7 +191,10 @@
             to_plane.append(c)
         else:
             acc[...] = both
-    out_d[0] = lax.dot_general(hidden, ys[...], (((0,), (0,)), ((), ())), preferred_element_type=F32).astype(BF)
+    over = lax.dot_general(xs[...], d_pre, (((0,), (0,)), ((), ())), preferred_element_type=F32)
+    gus[0] = over.astype(BF)
+    w_gu = pltpu.make_async_copy(gus, out_gu, ld.at[5])
+    w_gu.start()
     for i in range(3):
         to_plane[i].wait_recv()
         acc[...] += rb2[i].astype(F32)
@@ -218,6 +222,8 @@
     grad_in = table[...] * gain[...]
     d_rows = inverse * (grad_in - scaled * jnp.mean(grad_in * scaled, axis=1, keepdims=True))
     out_rows[...] = d_rows
+    w_d.wait()
+    w_gu.wait()
 
 
 def finish(rows, sel, gu, dn, out_lat, out_gu, out_d, sem):
@@ -257,9 +263,10 @@
             jax.ShapeDtypeStruct(w_down.shape, BF),
         ),
         in_specs=[any_, any_, vms, vms, vms, any_, any_],
-        out_specs=(vms,) * 4,
+        out_specs=(vms, vms, any_, any_),
         scratch_shapes=[
-            vm(latent.shape, BF), vm(dout.shape, BF), vm(w_gate_up.shape, BF), vm(w_down.shape, BF), dma((4,)),
+            vm(latent.shape, BF), vm(dout.shape, BF), vm(w_gate_up.shape, BF), vm(w_down.shape, BF),
+            vm(w_gate_up.shape, BF), vm(w_down.shape, BF), dma((6,)),
             vm((nr, width), F32), vm((nr, width), F32),
             vm((slots, 16, dw // 2), BF), vm((16, dw // 2), F32),
             vm((SLICES, slots, 16, dw // 2), BF),
@@ -280,7 +287,7 @@
             jax.ShapeDtypeStruct(w_gate_up.shape, BF),
             jax.ShapeDtypeStruct(w_down.shape, BF),
         ),
-        in_specs=[vms, vms, any_, any_],
+        in_specs=[vms] * 4,
         out_specs=(vms, any_, any_),
         scratch_shapes=[dma((2,))],
         compiler_params=pltpu.CompilerParams(vmem_limit_bytes=60 * 1024 * 1024),

time: 86.5 us -> 39.1 us (0.45)
  Pallas kernels: 85.6 us -> 38.2 us
    pallas_call x1, Pallas kernels: 50.6 us -> 3.56 us  [body(): pl.pallas_call(finish, out_shape=(jax.ShapeDtypeStruct(latent.shape, BF),...]
where the time goes in v3:
time: 39.1 us; the launch traced here: 38.8 us
  Pallas kernels  38.2 us (98%)
  between operations  0.64 us (2%)
    pallas_call x1, Pallas kernels, body(): pl.pallas_call(functools.partial(kernel, n_dp, groups), out_shape=(jax.Sh...  34.6 us
    pallas_call x1, Pallas kernels, body(): pl.pallas_call(finish, out_shape=(jax.ShapeDtypeStruct(latent.shape, BF),...  3.56 us

profile of v3, /device:TPU:0, one launch (start us, length us, event | category | flops | bytes accessed | tf_op | source)
XLA Modules:
  0.0 38.8 jit_solution(4221843717703764785)
XLA Ops:
  0.6 34.6 %shard_map.94 = (f32[8,4096]{1,0:T(8,128)}, f32[8,128]{1,0:T(8,128)}, bf16[1,2048,256]{2,1,0:T(8,128)(2,1)}, bf16[1,128,2048]{2,1,0:T(8,128)(2,1)}) custom-call(bf16[128,4096]{1,0:T(8,128)(2,1)} %lat_h.1, bf16[128,4096]{1,0:T(8,128)(2,1)} %dout_h.1, s32[2,128]{1,0:T(2,128)} %bitcast.4, f32[2,128]{1,0:T(2,128)} %bitcast.5, f32[1,4096]{1,0:T(1,128)} %bitcast.3, ...), custom_call_target="tpu_custom_call" | custom-call | tf_op jit(solution)/shard_map/pallas_call | solution.py:257
  35.3 3.6 %shard_map.95 = (bf16[128,4096]{1,0:T(8,128)(2,1)}, bf16[1,2048,256]{2,1,0:T(8,128)(2,1)}, bf16[1,128,2048]{2,1,0:T(8,128)(2,1)}) custom-call(f32[8,4096]{1,0:T(8,128)} %get-tuple-element.7.rows, f32[8,128]{1,0:T(8,128)} %get-tuple-element.8.sel, bf16[1,2048,256]{2,1,0:T(8,128)(2,1)} %get-tuple-element.9.gu, bf16[1,128,2048]{2,1,0:T(8,128)(2,1)} %get-tuple-element.10.dn), custom_call_target="tpu_custom_call" | custom-call | tf_op jit(solution)/shard_map/pallas_call | solution.py:283

commit v4 on v3

--- a/solution.py
+++ b/solution.py
@@ -169,35 +169,37 @@
     d_gate = dh * up * sig * (1.0 + gate * (1.0 - sig))
     d_pre = jnp.concatenate([d_gate, dh * act], axis=1).astype(BF)
     rows_m = slots * CAP
-    bk[...] = lax.dot_general(d_pre, wgu[0], (((1,), (1,)), ((), ())),
-                              preferred_element_type=F32).astype(BF).reshape(SLICES, rows_m, dw)
     mine = planes + (m,)
     to_sib = []
-    for i in range(4):
-        c = rcopy(bk.at[mine[i] + f0], rb1.at[i], s4.at[i], r4.at[i], sib)
-        c.start()
-        to_sib.append(c)
-    dns[0] = lax.dot_general(hidden, ys[...], (((0,), (0,)), ((), ())), preferred_element_type=F32).astype(BF)
-    w_d = pltpu.make_async_copy(dns, out_d, ld.at[4])
-    w_d.start()
+    for h in range(2):
+        bk[h] = lax.dot_general(d_pre, wgu[0, h * half:(h + 1) * half, :], (((1,), (1,)), ((), ())),
+                                preferred_element_type=F32).astype(BF).reshape(SLICES, rows_m, half)
+        for i in range(4):
+            k = h * 4 + i
+            c = rcopy(bk.at[h, mine[i] + f0], rb1.at[h, i], s4.at[k], r4.at[k], sib)
+            c.start()
+            to_sib.append(c)
     to_plane = []
-    for i in range(4):
-        to_sib[i].wait_recv()
-        both = bk[mine[i]].astype(F32) + rb1[i].astype(F32)
-        if i < 3:
-            mid[i] = both.astype(BF)
-            c = rcopy(mid.at[i], rb2.at[i], s5.at[i], r5.at[i], plane_devs[i])
-            c.start()
-            to_plane.append(c)
-        else:
-            acc[...] = both
+    for h in range(2):
+        for i in range(4):
+            to_sib[h * 4 + i].wait_recv()
+            both = bk[h, mine[i]].astype(F32) + rb1[h, i].astype(F32)
+            if i < 3:
+                k = h * 3 + i
+                mid[h, i] = both.astype(BF)
+                c = rcopy(mid.at[h, i], rb2.at[h, i], s5.at[k], r5.at[k], plane_devs[i])
+                c.start()
+                to_plane.append(c)
+            else:
+                acc[:, h * half:(h + 1) * half] = both
     over = lax.dot_general(xs[...], d_pre, (((0,), (0,)), ((), ())), preferred_element_type=F32)
     gus[0] = over.astype(BF)
     w_gu = pltpu.make_async_copy(gus, out_gu, ld.at[5])
     w_gu.start()
-    for i in range(3):
-        to_plane[i].wait_recv()
-        acc[...] += rb2[i].astype(F32)
+    for h in range(2):
+        for i in range(3):
+            to_plane[h * 3 + i].wait_recv()
+            acc[:, h * half:(h + 1) * half] += rb2[h, i].astype(F32)
     for s in range(slots):
         for q in range(4):
             homest[CAP * q:CAP * (q + 1), :] = acc[CAP * s:CAP * (s + 1), q * quarter:(q + 1) * quarter]
@@ -209,6 +211,9 @@
         c.start()
         home.append(c)
     fin[ms] = homeb[ms]
+    dns[0] = lax.dot_general(hidden, ys[...], (((0,), (0,)), ((), ())), preferred_element_type=F32).astype(BF)
+    w_d = pltpu.make_async_copy(dns, out_d, ld.at[4])
+    w_d.start()
     for c in xch + to_sib + to_plane:
         c.wait_send()
     for c in home:
@@ -226,15 +231,31 @@
     w_gu.wait()
 
 
-def finish(rows, sel, gu, dn, out_lat, out_gu, out_d, sem):
-    a = pltpu.make_async_copy(gu, out_gu, sem.at[0])
-    b = pltpu.make_async_copy(dn, out_d, sem.at[1])
-    a.start()
-    b.start()
-    out_lat[...] = lax.dot_general(sel[...].astype(BF), rows[...].astype(BF), (((0,), (0,)), ((), ())),
-                                   preferred_element_type=F32).astype(BF)
-    a.wait()
-    b.wait()
+def finish(rows, sel, gu, dn, out_lat, out_gu, out_d, gus, dns, lts, sem):
+    cut = gu.shape[1] // 2
+    wide = lts.shape[2]
+    plan = []
+    for k in range(2):
+        at = pl.ds(k * cut, cut)
+        plan.append((gu.at[:, at], gus.at[:, at], out_gu.at[:, at]))
+    plan.append((dn, dns, out_d))
+    loads = [pltpu.make_async_copy(a, b, sem.at[k]) for k, (a, b, _) in enumerate(plan)]
+    stores = [pltpu.make_async_copy(b, c, sem.at[3 + k]) for k, (_, b, c) in enumerate(plan)]
+    for c in loads:
+        c.start()
+    put = sel[...].astype(BF)
+    for k in range(4):
+        at = pl.ds(k * wide, wide)
+        lts[k] = lax.dot_general(put, rows[:, at].astype(BF), (((0,), (0,)), ((), ())),
+                                 preferred_element_type=F32).astype(BF)
+        c = pltpu.make_async_copy(lts.at[k], out_lat.at[:, at], sem.at[6 + k])
+        c.start()
+        stores.append(c)
+        if k < 3:
+            loads[k].wait()
+            stores[k].start()
+    for c in stores:
+        c.wait()
 
 
 def body(latent, dout, routes, gate_w, norm_gain, w_gate_up, w_down):
@@ -250,7 +271,7 @@
     vm = pltpu.VMEM
     dma = pltpu.SemaphoreType.DMA
     pairs = []
-    for n in (slots, 3 * slots, 4, 4 * max(n_dp - 1, 1), 4, 3, slots):
+    for n in (slots, 3 * slots, 4, 4 * max(n_dp - 1, 1), 8, 6, slots):
         pairs += [dma((n,)), dma((n,))]
     any_ = pl.BlockSpec(memory_space=pl.ANY)
     vms = pl.BlockSpec(memory_space=vm)
@@ -272,8 +293,8 @@
             vm((SLICES, slots, 16, dw // 2), BF),
             vm((rows, dw), BF), vm((rows, dw), BF),
             vm((4, rows // 4, 3 * hid), F32), vm((max(n_dp - 1, 1), 4, rows // 4, 3 * hid), F32),
-            vm((SLICES, rows_m, dw), BF), vm((4, rows_m, dw), BF), vm((3, rows_m, dw), BF),
-            vm((rows_m, dw), F32), vm((3, rows_m, dw), BF),
+            vm((2, SLICES, rows_m, dw // 2), BF), vm((2, 4, rows_m, dw // 2), BF), vm((2, 3, rows_m, dw // 2), BF),
+            vm((rows_m, dw), F32), vm((2, 3, rows_m, dw // 2), BF),
             vm((16, dw // 4), F32), vm((slots, 16, dw // 4), BF), vm((slots, 16, dw // 4), BF),
             vm((nr, width), F32),
         ] + pairs,
@@ -287,9 +308,9 @@
             jax.ShapeDtypeStruct(w_gate_up.shape, BF),
             jax.ShapeDtypeStruct(w_down.shape, BF),
         ),
-        in_specs=[vms] * 4,
-        out_specs=(vms, any_, any_),
-        scratch_shapes=[dma((2,))],
+        in_specs=[vms, vms, any_, any_],
+        out_specs=(any_,) * 3,
+        scratch_shapes=[vm(w_gate_up.shape, BF), vm(w_down.shape, BF), vm((4, patches, width // 4), BF), dma((10,))],
         compiler_params=pltpu.CompilerParams(vmem_limit_bytes=60 * 1024 * 1024),
     )(d_rows, sel, gu, dn)
 

time: 39.1 us -> 38.8 us (level)
  no operation moved by 1% of the time
where the time goes in v4:
time: 38.8 us; the launch traced here: 38.6 us
  Pallas kernels  37.9 us (98%)
  between operations  0.64 us (2%)
    pallas_call x1, Pallas kernels, body(): pl.pallas_call(functools.partial(kernel, n_dp, groups), out_shape=(jax.Sh...  34.5 us
    pallas_call x1, Pallas kernels, body(): pl.pallas_call(finish, out_shape=(jax.ShapeDtypeStruct(latent.shape, BF),...  3.45 us

profile of v4, /device:TPU:0, one launch (start us, length us, event | category | flops | bytes accessed | tf_op | source)
XLA Modules:
  0.0 38.6 jit_solution(7349939630308856814)
XLA Ops:
  0.6 34.5 %shard_map.94 = (f32[8,4096]{1,0:T(8,128)}, f32[8,128]{1,0:T(8,128)}, bf16[1,2048,256]{2,1,0:T(8,128)(2,1)}, bf16[1,128,2048]{2,1,0:T(8,128)(2,1)}) custom-call(bf16[128,4096]{1,0:T(8,128)(2,1)} %lat_h.1, bf16[128,4096]{1,0:T(8,128)(2,1)} %dout_h.1, s32[2,128]{1,0:T(2,128)} %bitcast.4, f32[2,128]{1,0:T(2,128)} %bitcast.5, f32[1,4096]{1,0:T(1,128)} %bitcast.3, ...), custom_call_target="tpu_custom_call" | custom-call | tf_op jit(solution)/shard_map/pallas_call | solution.py:278
  35.1 3.5 %shard_map.95 = (bf16[128,4096]{1,0:T(8,128)(2,1)}, bf16[1,2048,256]{2,1,0:T(8,128)(2,1)}, bf16[1,128,2048]{2,1,0:T(8,128)(2,1)}) custom-call(f32[8,4096]{1,0:T(8,128)} %get-tuple-element.7.rows, f32[8,128]{1,0:T(8,128)} %get-tuple-element.8.sel, bf16[1,2048,256]{2,1,0:T(8,128)(2,1)} %get-tuple-element.9.gu, bf16[1,128,2048]{2,1,0:T(8,128)(2,1)} %get-tuple-element.10.dn), custom_call_target="tpu_custom_call" | custom-call | tf_op jit(solution)/shard_map/pallas_call | solution.py:304

commit v5 on v4

--- a/solution.py
+++ b/solution.py
@@ -80,11 +80,11 @@
     w_rows = jnp.sum(sel * weight, axis=1, keepdims=True)
     pick = sel.astype(BF)
     loads[0].wait()
-    loads[1].wait()
     raw = jnp.dot(pick, lat[...], preferred_element_type=F32)
     inverse = lax.rsqrt(jnp.mean(raw * raw, axis=1, keepdims=True) + EPS)
     scaled = raw * inverse
     inrow[...] = scaled * gain[...]
+    loads[1].wait()
     dyrow[...] = w_rows * jnp.dot(pick, dout[...], preferred_element_type=F32)
     for dd in range(n_dp):
         for e in range(groups):
@@ -108,7 +108,7 @@
         at = (ms + slots - t) % slots
         if t:
             first[t - 1].wait_recv()
-        for i in range(3):
+        for i in (2, 0, 1):
             c = rcopy(gath.at[m, at], gath.at[m, at], s2.at[i * slots + t], r2.at[i * slots + t], plane_devs[i])
             c.start()
             sends.append((i, c))
@@ -142,7 +142,8 @@
             relay.append(c)
         relay[n].wait_recv()
         pair = (planes[n - 1] if n else m) // 2
-        lax.fori_loop(pair * 2 * per, pair * 2 * per + 2 * per, arrange, 0)
+        for k in range(2 * per):
+            arrange(pair * 2 * per + k, 0)
         if n == 0:
             loads[2].wait()
             loads[3].wait()

time: 38.8 us -> 38.5 us (level)
  no operation moved by 1% of the time
where the time goes in v5:
time: 38.5 us; the launch traced here: 38.2 us
  Pallas kernels  37.6 us (98%)
  between operations  0.64 us (2%)
    pallas_call x1, Pallas kernels, body(): pl.pallas_call(functools.partial(kernel, n_dp, groups), out_shape=(jax.Sh...  34.1 us
    pallas_call x1, Pallas kernels, body(): pl.pallas_call(finish, out_shape=(jax.ShapeDtypeStruct(latent.shape, BF),...  3.45 us

profile of v5, /device:TPU:0, one launch (start us, length us, event | category | flops | bytes accessed | tf_op | source)
XLA Modules:
  0.0 38.2 jit_solution(11117643253827995138)
XLA Ops:
  0.6 34.1 %shard_map.94 = (f32[8,4096]{1,0:T(8,128)}, f32[8,128]{1,0:T(8,128)}, bf16[1,2048,256]{2,1,0:T(8,128)(2,1)}, bf16[1,128,2048]{2,1,0:T(8,128)(2,1)}) custom-call(bf16[128,4096]{1,0:T(8,128)(2,1)} %lat_h.1, bf16[128,4096]{1,0:T(8,128)(2,1)} %dout_h.1, s32[2,128]{1,0:T(2,128)} %bitcast.4, f32[2,128]{1,0:T(2,128)} %bitcast.5, f32[1,4096]{1,0:T(1,128)} %bitcast.3, ...), custom_call_target="tpu_custom_call" | custom-call | tf_op jit(solution)/shard_map/pallas_call | solution.py:279
  34.8 3.5 %shard_map.95 = (bf16[128,4096]{1,0:T(8,128)(2,1)}, bf16[1,2048,256]{2,1,0:T(8,128)(2,1)}, bf16[1,128,2048]{2,1,0:T(8,128)(2,1)}) custom-call(f32[8,4096]{1,0:T(8,128)} %get-tuple-element.7.rows, f32[8,128]{1,0:T(8,128)} %get-tuple-element.8.sel, bf16[1,2048,256]{2,1,0:T(8,128)(2,1)} %get-tuple-element.9.gu, bf16[1,128,2048]{2,1,0:T(8,128)(2,1)} %get-tuple-element.10.dn), custom_call_target="tpu_custom_call" | custom-call | tf_op jit(solution)/shard_map/pallas_call | solution.py:305
